TPU v7x, 32 devices: a whole 2x2x4 slice. The times are simulated.
32 devices in a mesh: groups: 2 (over y), row: 4 (over z), col: 4 (over x, core).
Axes of the slice: x: 2, y: 2, z: 4, core: 2. Of those that a mesh axis runs over, the one named last changes fastest.
Arguments:
- node_embed: bfloat16 [384, 256], P(('groups', 'row')), parts along dimension 0, may hold values from -6 to 6
- rotation: float32 [3, 3, 384], P(None, None, 'groups'), parts along dimension 2, may hold values from -1 to 1, as said below
- translation: float32 [3, 384], P(None, 'groups'), parts along dimension 1, may hold values from -8 to 8
- pair_embed: bfloat16 [384, 192, 128], P(('groups', 'row'), 'col'), parts along dimension 0, may hold values from -1300 to 1300
- chain_index: int32 [384], P('groups'), parts along dimension 0, may hold values from 0 to 7, never falling along the last dimension, each value on 1 to 48 neighbouring positions
- residue_mask: int32 [384], P('groups'), parts along dimension 0, may hold values 0 or 1
- step_index: int32 [2], P('groups'), parts along dimension 0, may hold values from 0 to 999
- w_time: bfloat16 [256, 256], replicated, may hold values from -0.375 to 0.375
- w_query: bfloat16 [256, 2048], replicated, may hold values from -0.375 to 0.375
- w_query_points: bfloat16 [256, 192], replicated, may hold values from -0.375 to 0.375
- w_kv: bfloat16 [256, 4096], replicated, may hold values from -0.375 to 0.375
- w_kvp: bfloat16 [256, 480], replicated, may hold values from -0.375 to 0.375
- w_bias: bfloat16 [128, 8], replicated, may hold values from -0.5 to 0.5
- head_weights: float32 [8], replicated, may hold values from -1 to 1.5
- chain_bias: float32 [8], replicated, may hold values from -2 to 2
- w_out: bfloat16 [3456, 256], replicated, may hold values from -0.109375 to 0.109375
- w_mlp_in: bfloat16 [256, 256], replicated, may hold values from -0.375 to 0.375
- w_mlp_out: bfloat16 [256, 256], replicated, may hold values from -0.375 to 0.375
- w_edge_in: bfloat16 [256, 128], replicated, may hold values from -0.375 to 0.375
- w_trunk_in: bfloat16 [384, 384], replicated, may hold values from -0.3125 to 0.3125
- w_trunk_mid: bfloat16 [384, 384], replicated, may hold values from -0.3125 to 0.3125
- w_final: bfloat16 [384, 128], replicated, may hold values from -0.3125 to 0.3125
Outputs:
- node_out: bfloat16 [384, 256], P(('groups', 'row')), parts along dimension 0
- pair_out: bfloat16 [384, 192, 128], P(('groups', 'row'), 'col'), parts along dimension 0
There are 2 independent parts, one for each index of `groups`. A program takes and returns all parts, laid end to end along the dimension named above; an argument that names none is the same for every part. Nothing has to cross between parts.
Inputs may be any that keep to these rules, and one draw needn't show every extreme that they name: Each rotation[:, :, n] is a proper rotation matrix. `chain_index`: chain ids never fall along the residues; each chain has 1 to 48 residues, one exactly that many.
All inputs are finite; a program needn't handle non-finite values.
Results may differ from a plain program's by a relative error of at most 0.012.
Values may be sent and summed in bfloat16 or wider, within the bound.
No kernel may reach another device: no remote copies, remote signals or barrier semaphores. Data moves between devices by JAX's collectives and lax.ppermute only.
A program may use at most 64 MiB of HBM per device.

v0:
```python
import math
import jax
import jax.numpy as jnp
from jax import lax
from jax.sharding import PartitionSpec as P

CS = 256
CZ = 128
HEADS = 8
CH = 256
QP = 8
VP = 12
NH = 128
HID = 384
norm_epsilon = 1e-05
masked_score = 100000.0
highest = lax.Precision.HIGHEST


def layer_norm(values):
    average = jnp.mean(values, -1, keepdims=True)
    centred = values - average
    spread = jnp.mean(centred * centred, -1, keepdims=True)
    return centred * lax.rsqrt(spread + norm_epsilon)


def time_embedding(step_index, embed_width):
    half_width = embed_width // 2
    frequency = jnp.exp(-math.log(10000.0) * jnp.arange(half_width, dtype=jnp.float32) / half_width)
    angles = step_index.astype(jnp.float32)[0] * frequency
    return jnp.concatenate([jnp.sin(angles), jnp.cos(angles)])[None, :].astype(jnp.bfloat16)


def to_global(rotation, shift_vec, points):
    turned = jnp.einsum("abn,nbm->nam", rotation, points, precision=highest)
    return turned + jnp.transpose(shift_vec)[:, :, None]


def project_keys(embedded, rotation, shift_vec, w_kv, w_kvp):
    item_count = embedded.shape[0]
    key_values = jnp.dot(embedded, w_kv, preferred_element_type=jnp.float32).astype(jnp.bfloat16)
    points = jnp.dot(embedded, w_kvp, preferred_element_type=jnp.float32).reshape(item_count, 3, -1)
    return (key_values, to_global(rotation, shift_vec, points))


def node_finish(
    denominator,
    values_out,
    points_out,
    pair_sums,
    embedded,
    rotation,
    shift_vec,
    mask_rows,
    w_out,
    w_mlp_in,
    w_mlp_out,
    w_edge_in,
):
    item_count = embedded.shape[0]
    scale_back = denominator[:, :, None]
    attended = values_out.reshape(item_count, HEADS, CH) / scale_back
    points = points_out.reshape(item_count, 3, HEADS, VP) / denominator[:, None, :, None]
    relative = points - jnp.transpose(shift_vec)[:, :, None, None]
    framed = jnp.einsum("abi,iahv->ibhv", rotation, relative, precision=highest)
    length = jnp.sqrt(jnp.maximum(jnp.sum(framed * framed, 1), 1.0))
    paired = pair_sums.reshape(item_count, HEADS, CZ) / scale_back
    features = jnp.concatenate(
        [
            attended.reshape(item_count, -1),
            framed.reshape(item_count, -1),
            length.reshape(item_count, -1),
            paired.reshape(item_count, -1),
        ],
        -1,
    ).astype(jnp.bfloat16)
    update = jnp.dot(features, w_out, preferred_element_type=jnp.float32)
    normed = layer_norm(embedded.astype(jnp.float32) + update).astype(jnp.bfloat16)
    normed = lax.optimization_barrier(normed)
    middle = jax.nn.relu(jnp.dot(normed, w_mlp_in, preferred_element_type=jnp.float32)).astype(
        jnp.bfloat16
    )
    node_new = layer_norm(
        normed.astype(jnp.float32) + jnp.dot(middle, w_mlp_out, preferred_element_type=jnp.float32)
    )
    node_new = (node_new * mask_rows.astype(jnp.float32)[:, None]).astype(jnp.bfloat16)
    edge_side = jnp.dot(node_new, w_edge_in, preferred_element_type=jnp.float32).astype(
        jnp.bfloat16
    )
    return (node_new, edge_side)


def body(
    node_embed,
    rotation,
    translation,
    pair_embed,
    chain_index,
    residue_mask,
    step_index,
    w_time,
    w_query,
    w_query_points,
    w_kv,
    w_kvp,
    w_bias,
    head_weights,
    chain_bias,
    w_out,
    w_mlp_in,
    w_mlp_out,
    w_edge_in,
    w_trunk_in,
    w_trunk_mid,
    w_final,
):
    row_count = node_embed.shape[0]
    key_count = pair_embed.shape[1]
    row_start = lax.axis_index("row") * row_count
    key_start = lax.axis_index("col") * key_count
    embedded = (
        node_embed.astype(jnp.float32)
        + jnp.dot(time_embedding(step_index, CS), w_time, preferred_element_type=jnp.float32)
    ).astype(jnp.bfloat16)
    embedded = lax.optimization_barrier(embedded)
    rot_rows = lax.dynamic_slice_in_dim(rotation, row_start, row_count, 2)
    shift_rows = lax.dynamic_slice_in_dim(translation, row_start, row_count, 1)
    mask_rows = lax.dynamic_slice_in_dim(residue_mask, row_start, row_count, 0)
    mask_keys = lax.dynamic_slice_in_dim(residue_mask, key_start, key_count, 0)
    chain_rows = lax.dynamic_slice_in_dim(chain_index, row_start, row_count, 0)
    chain_keys = lax.dynamic_slice_in_dim(chain_index, key_start, key_count, 0)
    query_feat = (
        jnp.dot(embedded, w_query, preferred_element_type=jnp.float32)
        .astype(jnp.bfloat16)
        .reshape(row_count, HEADS, CH)
    )
    query_pts = to_global(
        rot_rows,
        shift_rows,
        jnp.dot(embedded, w_query_points, preferred_element_type=jnp.float32).reshape(
            row_count, 3, HEADS * QP
        ),
    ).reshape(row_count, 3, HEADS, QP)
    all_nodes = lax.all_gather(embedded, "row", axis=0, tiled=True)
    key_nodes = lax.dynamic_slice_in_dim(all_nodes, key_start, key_count, 0)
    rot_keys = lax.dynamic_slice_in_dim(rotation, key_start, key_count, 2)
    shift_keys = lax.dynamic_slice_in_dim(translation, key_start, key_count, 1)
    key_values, key_points = project_keys(key_nodes, rot_keys, shift_keys, w_kv, w_kvp)
    key_feat = key_values[:, : HEADS * CH].reshape(key_count, HEADS, CH)
    value_feat = key_values[:, HEADS * CH :].reshape(key_count, HEADS, CH)
    key_points = key_points.reshape(key_count, 3, HEADS, QP + VP)
    key_pts = key_points[..., :QP]
    value_pts = key_points[..., QP:]
    scaled = math.sqrt(1.0 / 3.0)
    point_weight = math.sqrt(2.0 / (9.0 * QP))
    point_gain = jax.nn.softplus(head_weights)
    feature_dots = jnp.einsum(
        "ihc,jhc->hij", query_feat, key_feat, preferred_element_type=jnp.float32
    ) / math.sqrt(CH)
    pair_bias = jnp.einsum("ijc,ch->hij", pair_embed, w_bias, preferred_element_type=jnp.float32)
    same_chain = (chain_rows[:, None] == chain_keys[None, :]).astype(jnp.float32)
    query_square = jnp.einsum("iahp,iahp->hi", query_pts, query_pts, precision=highest)
    key_square = jnp.einsum("jahp,jahp->hj", key_pts, key_pts, precision=highest)
    cross_term = jnp.einsum("iahp,jahp->hij", query_pts, key_pts, precision=highest)
    distance = query_square[:, :, None] + key_square[:, None, :] - 2.0 * cross_term
    mask_term = (mask_keys.astype(jnp.float32) - 1.0) * masked_score
    scores = (
        scaled * (feature_dots + pair_bias + chain_bias[:, None, None] * same_chain[None])
        - scaled * point_weight * 0.5 * point_gain[:, None, None] * distance
        + mask_term[None, None, :]
    )
    row_peak = lax.pmax(jnp.max(scores, -1), "col")
    weights = jnp.exp(scores - row_peak[:, :, None])
    denominator = jnp.transpose(jnp.sum(weights, -1))
    rounded = weights.astype(jnp.bfloat16)
    values_out = jnp.einsum(
        "hij,jhc->ihc", rounded, value_feat, preferred_element_type=jnp.float32
    ).reshape(row_count, -1)
    points_out = jnp.einsum("hij,jahv->iahv", weights, value_pts, precision=highest).reshape(
        row_count, -1
    )
    pair_sums = jnp.einsum(
        "hij,ijc->ihc", rounded, pair_embed, preferred_element_type=jnp.float32
    ).reshape(row_count, -1)
    summed = lax.psum((denominator, values_out, points_out, pair_sums), "col")
    node_out, edge_side = node_finish(
        summed[0],
        summed[1],
        summed[2],
        summed[3],
        embedded,
        rot_rows,
        shift_rows,
        mask_rows,
        w_out,
        w_mlp_in,
        w_mlp_out,
        w_edge_in,
    )
    side_all = lax.all_gather(edge_side, "row", axis=0, tiled=True)
    side_rows = lax.dynamic_slice_in_dim(side_all, row_start, row_count, 0)
    side_keys = lax.dynamic_slice_in_dim(side_all, key_start, key_count, 0)
    pre_rows = jnp.dot(side_rows, w_trunk_in[CZ : CZ + NH], preferred_element_type=jnp.float32)
    pre_keys = jnp.dot(side_keys, w_trunk_in[CZ + NH :], preferred_element_type=jnp.float32)
    mask_key_f = mask_keys.astype(jnp.float32)
    block_rows = math.gcd(row_count, 8)
    block_count = row_count // block_rows

    def edge_block(inputs):
        pair_block, pre_block, side_block, keep_block = inputs
        lifted = (
            jnp.einsum(
                "ijc,cd->ijd", pair_block, w_trunk_in[:CZ], preferred_element_type=jnp.float32
            )
            + pre_block[:, None, :]
            + pre_keys[None, :, :]
        )
        hidden_one = jax.nn.relu(lifted).astype(jnp.bfloat16)
        hidden_two = jax.nn.relu(
            jnp.einsum("ijd,de->ije", hidden_one, w_trunk_mid, preferred_element_type=jnp.float32)
        )
        stacked = jnp.concatenate(
            [
                pair_block,
                jnp.broadcast_to(side_block[:, None, :], (block_rows, key_count, NH)),
                jnp.broadcast_to(side_keys[None, :, :], (block_rows, key_count, NH)),
            ],
            -1,
        )
        joined = (hidden_two + stacked.astype(jnp.float32)).astype(jnp.bfloat16)
        edge_out = jnp.einsum("ijd,dc->ijc", joined, w_final, preferred_element_type=jnp.float32)
        pair_keep = keep_block.astype(jnp.float32)[:, None] * mask_key_f[None, :]
        return (layer_norm(edge_out) * pair_keep[:, :, None]).astype(jnp.bfloat16)

    pair_out = lax.map(
        edge_block,
        (
            pair_embed.reshape(block_count, block_rows, key_count, CZ),
            pre_rows.reshape(block_count, block_rows, HID),
            side_rows.reshape(block_count, block_rows, NH),
            mask_rows.reshape(block_count, block_rows),
        ),
    )
    return (node_out, pair_out.reshape(row_count, key_count, CZ))


def solution(mesh):
    return jax.shard_map(
        body,
        mesh=mesh,
        in_specs=(
            P(("groups", "row"), None),
            P(None, None, "groups"),
            P(None, "groups"),
            P(("groups", "row"), "col", None),
            P("groups"),
            P("groups"),
            P("groups"),
            P(),
            P(),
            P(),
            P(),
            P(),
            P(),
            P(),
            P(),
            P(),
            P(),
            P(),
            P(),
            P(),
            P(),
            P(),
        ),
        out_specs=(P(("groups", "row"), None), P(("groups", "row"), "col", None)),
        check_vma=False,
    )
```

profile of v0, /device:TPU:0, one launch (start us, length us, event | category | flops | bytes accessed | tf_op | source)
XLA Modules:
  0.0 135.2 jit_solution(5228488410972986476)
XLA Ops:
  8.0 1.2 fusion.59
  9.3 1.3 add_multiply_fusion
  10.6 1.4 %fusion.61 = (f32[48]{0:T(128)}, s32[48]{0:T(128)}, s32[48]{0:T(128)}, s32[48]{0:T(128)}) fusion(s32[192]{0:T(256)} %param.29, s32[]{:T(128)S(6)} %select_n.8, s32[192]{0:T(256)} %param.28, s32[]{:T(128)S(6)} %select_n.7), kind=kLoop, calls=%fused_computation.115 | loop fusion | flops 48 | bytes 1352 | tf_op jit(solution)/shard_map/convert_element_type | solution.py:86
  13.8 1.0 fusion.68
  15.7 15.0 %all_gather.6 = bf16[192,256]{1,0:T(8,128)(2,1)S(1)} all-gather(bf16[48,256]{1,0:T(8,128)(2,1)S(1)} %add_convert_fusion), channel_id=1, replica_groups=mesh['groups'=2,'row'=4,'col'=4] {'row'}, dimensions={0}, use_global_device_ids=true | all-gather | bytes 122880 | tf_op jit(solution)/shard_map/all_gather | solution.py:144
  30.7 1.1 fusion.69
  33.4 1.1 fusion.50
  35.4 1.5 %convolution_convert_fusion.1 = bf16[48,2048]{1,0:T(8,128)(2,1)S(1)} fusion(bf16[48,256]{1,0:T(8,128)(2,1)S(1)} %add_convert_fusion, bf16[256,2048]{1,0:T(8,128)(2,1)} %param.32), kind=kOutput, calls=%fused_computation.30 | convolution fusion | flops 50429952 | bytes 1269760 | tf_op jit(solution)/shard_map/dot_general | solution.py:133
  37.0 1.3 fusion.54
  39.1 1.3 convolution_convert_fusion
  41.2 1.1 fusion.27
  42.6 5.7 %pmax.7 = f32[8,48]{1,0:T(8,128)S(1)} all-reduce(f32[8,48]{1,0:T(8,128)S(1)} %get-tuple-element.115), channel_id=1, replica_groups=mesh['groups'=2,'row'=4,'col'=4] {'col'}, use_global_device_ids=true, to_apply=%region_1.2 | all-reduce | flops 384 | bytes 3072 | tf_op jit(solution)/shard_map/pmax | solution.py:172
  48.5 1.2 convolution_bitcast_fusion
  51.8 15.2 %all-reduce = (f32[48,8]{0,1:T(8,128)S(1)}, f32[48,3,8,12]{0,3,1,2:T(8,128)S(1)}) all-reduce(f32[48,8]{0,1:T(8,128)S(1)} %bitcast.172, f32[48,3,8,12]{0,3,1,2:T(8,128)S(1)} %convolution_bitcast_fusion.1), channel_id=1, replica_groups=mesh['groups'=2,'row'=4,'col'=4] {'col'}, use_global_device_ids=true, to_apply=%region_4.5 | all-reduce | flops 14208 | bytes 113664 | tf_op jit(solution)/shard_map/psum | solution.py:185
  67.7 1.8 %copy.97 = f32[48,3,8,12]{3,1,2,0:T(4,128)S(1)} copy(f32[48,3,8,12]{0,3,1,2:T(8,128)} %divide_subtract_fusion) | data formatting | bytes 110592 | tf_op jit(solution)/shard_map/sub | solution.py:64
  69.5 4.5 %multiply_reduce_fusion.1 = (f32[48,8,12]{2,1,0:T(8,128)}, bf16[48,3,8,12]{3,1,2,0:T(4,128)(2,1)}) fusion(f32[48,3,8,12]{3,1,2,0:T(4,128)S(1)} %copy.97, f32[3,3,48]{1,0,2:T(4,128)} %copy-done.4), kind=kOutput, calls=%fused_computation.51 | convolution fusion | flops 534528 | bytes 103104 | tf_op jit(solution)/shard_map/abi,iahv->ibhv/dot_general | solution.py:65
  74.4 1.1 copy.99
  75.6 1.5 %copy.98 = bf16[48,3,8,12]{0,3,2,1:T(8,128)(2,1)S(1)} copy(bf16[48,3,8,12]{3,1,2,0:T(4,128)(2,1)} %get-tuple-element.102) | data formatting | bytes 55296 | tf_op jit(solution)/shard_map/convert.5
  77.2 10.0 %all-reduce.4.cloned.1.call-done = (f32[48,2048]{1,0:T(8,128)}, f32[48,1024]{1,0:T(8,128)}) async-done(((f32[48,2048]{1,0:T(8,128)}, f32[48,1024]{1,0:T(8,128)}), (f32[48,2048]{1,0:T(8,128)}, f32[48,1024]{1,0:T(8,128)})) %all-reduce.4.cloned.1.call-update) | async-done | bytes 589840 | tf_op jit(solution)/shard_map/psum | solution.py:185
  87.3 1.0 fusion.29
  88.3 1.1 divide_convert_fusion
  89.5 2.0 %fusion.66 = (f32[48]{0:T(128)S(1)}, f32[48,256]{1,0:T(8,128)S(1)}) fusion(bf16[48,3456]{1,0:T(8,128)(2,1)S(1)} %concatenate.14, bf16[3456,256]{1,0:T(8,128)(2,1)} %param.39, bf16[48,256]{1,0:T(8,128)(2,1)S(1)} %add_convert_fusion), kind=kOutput, calls=%fused_computation.120 | convolution fusion | flops 84971472 | bytes 2175168 | tf_op jit(solution)/shard_map/dot_general | solution.py:77
  93.5 13.2 %all_gather.7 = bf16[192,128]{1,0:T(8,128)(2,1)S(1)} all-gather(bf16[48,128]{1,0:T(8,128)(2,1)S(1)} %convolution_convert_fusion.2), channel_id=1, replica_groups=mesh['groups'=2,'row'=4,'col'=4] {'row'}, dimensions={0}, use_global_device_ids=true | all-gather | bytes 61440 | tf_op jit(solution)/shard_map/all_gather | solution.py:200
  106.7 1.0 convolution_bitcast_fusion.3
  107.7 1.7 %fusion.44 = f32[48,384]{1,0:T(8,128)} fusion(bf16[48,128]{1,0:T(8,128)(2,1)S(1)} %get-tuple-element.215, bf16[384,384]{1,0:T(8,128)(2,1)} %param.43), kind=kOutput, calls=%fused_computation.74 | convolution fusion | flops 4718592 | bytes 184320 | tf_op jit(solution)/shard_map/dot_general | solution.py:204
  109.4 18.9 %while.10 = (s32[]{:T(128)}, bf16[6,8,48,128]{3,2,1,0:T(8,128)(2,1)}, bf16[6,8,48,128]{3,2,1,0:T(8,128)(2,1)S(1)}, bf16[384,384]{1,0:T(8,128)(2,1)}, f32[6,8,384...) while((s32[]{:T(128)}, ...), condition=%wide.region_15.16_spmd, body=%wide.region_12.15_spmd.sunk | while | flops 191054592 | bytes 2702265 | solution.py:235
  109.5 1.5 %fusion.111 = bf16[8,48,384]{2,1,0:T(8,128)(2,1)S(1)} fusion(bf16[8,48,128]{2,1,0:T(8,128)(2,1)S(1)} %dynamic-slice_bitcast_fusion.9, bf16[8,48,128]{2,1,0:T(8,128)(2,1)S(1)} %broadcast_in_dim.14, bf16[8,48,128]{2,1,0:T(8,128)(2,1)S(1)} %broadcast_in_dim.15, bf16[384,384]{1,0:T(8,128)(2,1)} %get-tuple-element.239, f32[48,384]{1,0:T(8,128)} %get-tuple-element.238, ...), kind=kOutput, calls=%fused_computation.6.clone.1 | convolution fusion | flops 152911872 | bytes 1167360 | tf_op jit(solution)/shard_map/while/body/eval_jaxpr/ijd,de->ije/dot_general | solution.py:220
  112.7 1.5 %fusion.111 = bf16[8,48,384]{2,1,0:T(8,128)(2,1)S(1)} fusion(bf16[8,48,128]{2,1,0:T(8,128)(2,1)S(1)} %dynamic-slice_bitcast_fusion.9, bf16[8,48,128]{2,1,0:T(8,128)(2,1)S(1)} %broadcast_in_dim.14, bf16[8,48,128]{2,1,0:T(8,128)(2,1)S(1)} %broadcast_in_dim.15, bf16[384,384]{1,0:T(8,128)(2,1)} %get-tuple-element.239, f32[48,384]{1,0:T(8,128)} %get-tuple-element.238, ...), kind=kOutput, calls=%fused_computation.6.clone.1 | convolution fusion | flops 152911872 | bytes 1167360 | tf_op jit(solution)/shard_map/while/body/eval_jaxpr/ijd,de->ije/dot_general | solution.py:220
  115.8 1.5 %fusion.111 = bf16[8,48,384]{2,1,0:T(8,128)(2,1)S(1)} fusion(bf16[8,48,128]{2,1,0:T(8,128)(2,1)S(1)} %dynamic-slice_bitcast_fusion.9, bf16[8,48,128]{2,1,0:T(8,128)(2,1)S(1)} %broadcast_in_dim.14, bf16[8,48,128]{2,1,0:T(8,128)(2,1)S(1)} %broadcast_in_dim.15, bf16[384,384]{1,0:T(8,128)(2,1)} %get-tuple-element.239, f32[48,384]{1,0:T(8,128)} %get-tuple-element.238, ...), kind=kOutput, calls=%fused_computation.6.clone.1 | convolution fusion | flops 152911872 | bytes 1167360 | tf_op jit(solution)/shard_map/while/body/eval_jaxpr/ijd,de->ije/dot_general | solution.py:220
  119.0 1.5 %fusion.111 = bf16[8,48,384]{2,1,0:T(8,128)(2,1)S(1)} fusion(bf16[8,48,128]{2,1,0:T(8,128)(2,1)S(1)} %dynamic-slice_bitcast_fusion.9, bf16[8,48,128]{2,1,0:T(8,128)(2,1)S(1)} %broadcast_in_dim.14, bf16[8,48,128]{2,1,0:T(8,128)(2,1)S(1)} %broadcast_in_dim.15, bf16[384,384]{1,0:T(8,128)(2,1)} %get-tuple-element.239, f32[48,384]{1,0:T(8,128)} %get-tuple-element.238, ...), kind=kOutput, calls=%fused_computation.6.clone.1 | convolution fusion | flops 152911872 | bytes 1167360 | tf_op jit(solution)/shard_map/while/body/eval_jaxpr/ijd,de->ije/dot_general | solution.py:220
  122.1 1.5 %fusion.111 = bf16[8,48,384]{2,1,0:T(8,128)(2,1)S(1)} fusion(bf16[8,48,128]{2,1,0:T(8,128)(2,1)S(1)} %dynamic-slice_bitcast_fusion.9, bf16[8,48,128]{2,1,0:T(8,128)(2,1)S(1)} %broadcast_in_dim.14, bf16[8,48,128]{2,1,0:T(8,128)(2,1)S(1)} %broadcast_in_dim.15, bf16[384,384]{1,0:T(8,128)(2,1)} %get-tuple-element.239, f32[48,384]{1,0:T(8,128)} %get-tuple-element.238, ...), kind=kOutput, calls=%fused_computation.6.clone.1 | convolution fusion | flops 152911872 | bytes 1167360 | tf_op jit(solution)/shard_map/while/body/eval_jaxpr/ijd,de->ije/dot_general | solution.py:220
  125.3 1.5 %fusion.111 = bf16[8,48,384]{2,1,0:T(8,128)(2,1)S(1)} fusion(bf16[8,48,128]{2,1,0:T(8,128)(2,1)S(1)} %dynamic-slice_bitcast_fusion.9, bf16[8,48,128]{2,1,0:T(8,128)(2,1)S(1)} %broadcast_in_dim.14, bf16[8,48,128]{2,1,0:T(8,128)(2,1)S(1)} %broadcast_in_dim.15, bf16[384,384]{1,0:T(8,128)(2,1)} %get-tuple-element.239, f32[48,384]{1,0:T(8,128)} %get-tuple-element.238, ...), kind=kOutput, calls=%fused_computation.6.clone.1 | convolution fusion | flops 152911872 | bytes 1167360 | tf_op jit(solution)/shard_map/while/body/eval_jaxpr/ijd,de->ije/dot_general | solution.py:220
  (154 shorter events, 22.1 us)
Async XLA Ops:
  7.2 32.0 %copy-start = (bf16[256,4096]{1,0:T(8,128)(2,1)S(1)}, bf16[256,4096]{1,0:T(8,128)(2,1)}, u32[]{:S(2)}) copy-start(bf16[256,4096]{1,0:T(8,128)(2,1)} %param.34) | copy-start | bytes 6291460
  7.2 80.0 %all-reduce.4.cloned.1.call-start = ((), (), s32[]{:S(2)}) async-start(), calls=%async_computation | async-start | bytes 1179648 | tf_op jit(solution)/shard_map/psum | solution.py:185
  30.7 2.7 %copy-start.5 = (bf16[192,256]{1,0:T(8,128)(2,1)}, bf16[192,256]{1,0:T(8,128)(2,1)S(1)}, u32[]{:S(2)}) copy-start(bf16[192,256]{1,0:T(8,128)(2,1)S(1)} %all_gather.6) | copy-start | bytes 294916
  32.2 2.3 %copy-start.4 = (f32[3,3,48]{1,0,2:T(4,128)}, f32[3,3,48]{1,0,2:T(4,128)S(1)}, u32[]{:S(2)}) copy-start(f32[3,3,48]{1,0,2:T(4,128)S(1)} %copy.125) | copy-start | bytes 5188
  32.2 4.7 %copy-start.1 = (bf16[48,48,128]{2,1,0:T(8,128)(2,1)S(1)}, bf16[48,48,128]{2,1,0:T(8,128)(2,1)}, u32[]{:S(2)}) copy-start(bf16[48,48,128]{2,1,0:T(8,128)(2,1)} %param.27) | copy-start | bytes 1769476
  36.9 4.2 %copy-start.13 = (s32[48]{0:T(128)S(1)}, s32[48]{0:T(128)}, u32[]{:S(2)}) copy-start(s32[48]{0:T(128)} %get-tuple-element.122) | copy-start | bytes 580
  36.9 4.2 %copy-start.14 = (s32[48]{0:T(128)S(1)}, s32[48]{0:T(128)}, u32[]{:S(2)}) copy-start(s32[48]{0:T(128)} %get-tuple-element.123) | copy-start | bytes 580
  36.9 4.2 %copy-start.9 = (f32[8,48]{1,0:T(8,128)S(1)}, f32[8,48]{1,0:T(8,128)}, u32[]{:S(2)}) copy-start(f32[8,48]{1,0:T(8,128)} %fusion.42) | copy-start | bytes 4612
  38.3 4.0 %copy-start.11 = (f32[48]{0:T(128)S(1)}, f32[48]{0:T(128)}, u32[]{:S(2)}) copy-start(f32[48]{0:T(128)} %get-tuple-element.95) | copy-start | bytes 580
  38.3 4.0 %copy-start.15 = (f32[8]{0:T(128)S(1)}, f32[8]{0:T(128)}, u32[]{:S(2)}) copy-start(f32[8]{0:T(128)} %param.38) | copy-start | bytes 100
  39.1 3.2 %copy-start.3 = (f32[8,48,48]{1,2,0:T(8,128)S(1)}, f32[8,48,48]{1,2,0:T(8,128)}, u32[]{:S(2)}) copy-start(f32[8,48,48]{1,2,0:T(8,128)} %copy.83) | copy-start | bytes 221188
  51.4 22.6 %copy-start.12 = (s32[48]{0:T(128)S(1)}, s32[48]{0:T(128)}, u32[]{:S(2)}) copy-start(s32[48]{0:T(128)} %get-tuple-element.94) | copy-start | bytes 580
  88.3 4.2 %copy-start.10 = (f32[48]{0:T(128)S(1)}, f32[48]{0:T(128)}, u32[]{:S(2)}) copy-start(f32[48]{0:T(128)} %get-tuple-element.93) | copy-start | bytes 580
  89.3 20.1 %copy-start.2 = (bf16[384,128]{1,0:T(8,128)(2,1)S(1)}, bf16[384,128]{1,0:T(8,128)(2,1)}, u32[]{:S(2)}) copy-start(bf16[384,128]{1,0:T(8,128)(2,1)} %param.45) | copy-start | bytes 294916
  89.5 2.4 %copy-start.6 = (bf16[256,256]{1,0:T(8,128)(2,1)S(1)}, bf16[256,256]{1,0:T(8,128)(2,1)}, u32[]{:S(2)}) copy-start(bf16[256,256]{1,0:T(8,128)(2,1)} %param.41) | copy-start | bytes 393220
  89.5 2.4 %copy-start.7 = (bf16[256,256]{1,0:T(8,128)(2,1)S(1)}, bf16[256,256]{1,0:T(8,128)(2,1)}, u32[]{:S(2)}) copy-start(bf16[256,256]{1,0:T(8,128)(2,1)} %param.40) | copy-start | bytes 393220
  92.5 16.9 %copy-start.8 = (bf16[48,256]{1,0:T(8,128)(2,1)}, bf16[48,256]{1,0:T(8,128)(2,1)S(1)}, u32[]{:S(2)}) copy-start(bf16[48,256]{1,0:T(8,128)(2,1)S(1)} %multiply_convert_fusion.1) | copy-start | bytes 73732
Sparse Core Ops, SparseCore 0:
  51.6 35.5 all-reduce.3
where the time goes:
time: 136 us; the launch traced here: 135 us
  blocking collectives  49.1 us (36%)
  matrix products  33.2 us (24%)
  other arithmetic  15.9 us (12%)
  between operations  15.3 us (11%)
  local copies, waits for them, and re-layouts  11.4 us (8%)
  waiting for transfers between devices  10 us (7%)
    psum x1, blocking collectives, body(): summed = lax.psum((denominator, values_out, points_out, pair_sums), 'col')  15.2 us
    all_gather x1, blocking collectives, body(): all_nodes = lax.all_gather(embedded, 'row', axis=0, tiled=True)  15 us
    all_gather x1, blocking collectives, body(): side_all = lax.all_gather(edge_side, 'row', axis=0, tiled=True)  13.2 us
    psum x1, waiting for transfers between devices, body(): summed = lax.psum((denominator, values_out, points_out, pair_sums), 'col')  9.98 us
    dot_general x6, matrix products, edge_block(): jnp.einsum('ijd,de->ije', hidden_one, w_trunk_mid, preferred_element_type...  9.25 us
    pmax x1, blocking collectives, body(): row_peak = lax.pmax(jnp.max(scores, -1), 'col')  5.67 us
    dynamic_update_slice x6, other arithmetic, body(): lax.map(edge_block, (pair_embed.reshape(block_count, block_rows, key_coun...  5.22 us
    dot_general x1, matrix products, node_finish(): framed = jnp.einsum('abi,iahv->ibhv', rotation, relative, precision=highest)  4.51 us
  transfers between devices with their start and end apart: 1, of which 1 were waited for; matrix products, arithmetic and copies ran while one was open for 8% of the time, Pallas kernels for 0%

commit v1 on v0

--- a/solution.py
+++ b/solution.py
@@ -15,6 +15,17 @@
 norm_epsilon = 1e-05
 masked_score = 100000.0
 highest = lax.Precision.HIGHEST
+
+
+def ring_gather(shard, axis, dim):
+    ways = lax.axis_size(axis)
+    pieces = [shard]
+    for far in range(1, ways):
+        pieces.append(
+            lax.ppermute(pieces[far - 1], axis, [(d, (d - 1) % ways) for d in range(ways)])
+        )
+    line = jnp.concatenate(pieces, axis=dim)
+    return jnp.roll(line, lax.axis_index(axis) * shard.shape[dim], axis=dim)
 
 
 def layer_norm(values):
@@ -141,7 +152,7 @@
             row_count, 3, HEADS * QP
         ),
     ).reshape(row_count, 3, HEADS, QP)
-    all_nodes = lax.all_gather(embedded, "row", axis=0, tiled=True)
+    all_nodes = ring_gather(embedded, "row", 0)
     key_nodes = lax.dynamic_slice_in_dim(all_nodes, key_start, key_count, 0)
     rot_keys = lax.dynamic_slice_in_dim(rotation, key_start, key_count, 2)
     shift_keys = lax.dynamic_slice_in_dim(translation, key_start, key_count, 1)

time: 136 us -> 146 us (1.074)
  waiting for transfers between devices: 10 us -> 32.1 us
  blocking collectives: 49.1 us -> 32.7 us
  starting transfers between devices: 0.04 us -> 7.74 us
  other arithmetic: 15.9 us -> 12.2 us
    psum x1, waiting for transfers between devices: 9.98 us -> 27.1 us  [body(): summed = lax.psum((denominator, values_out, points_out, pair_sums), 'col')]
    all_gather x1 -> x0, blocking collectives: 15 us -> none  [body(): all_nodes = lax.all_gather(embedded, 'row', axis=0, tiled=True)]
    ppermute x0 -> x3, starting transfers between devices: none -> 7.7 us  [ring_gather(): lax.ppermute(pieces[far - 1], axis, [(d, (d - 1) % ways) for d in range(w...]
    ppermute x0 -> x3, waiting for transfers between devices: none -> 4.99 us  [ring_gather(): lax.ppermute(pieces[far - 1], axis, [(d, (d - 1) % ways) for d in range(w...]
  transfers between devices with their start and end apart: 1 -> 4, of which waited for: 1 -> 3; matrix products, arithmetic and copies ran while one was open for 8% -> 11% of each run, Pallas kernels for 0% -> 0%
where the time goes in v1:
time: 146 us; the launch traced here: 145 us
  blocking collectives  32.7 us (22%)
  matrix products  32.6 us (22%)
  waiting for transfers between devices  32.1 us (22%)
  between operations  15.3 us (10%)
  other arithmetic  12.2 us (8%)
  local copies, waits for them, and re-layouts  12 us (8%)
  starting transfers between devices  7.74 us (5%)
    psum x1, waiting for transfers between devices, body(): summed = lax.psum((denominator, values_out, points_out, pair_sums), 'col')  27.1 us
    psum x1, blocking collectives, body(): summed = lax.psum((denominator, values_out, points_out, pair_sums), 'col')  13.8 us
    all_gather x1, blocking collectives, body(): side_all = lax.all_gather(edge_side, 'row', axis=0, tiled=True)  13.2 us
    dot_general x6, matrix products, edge_block(): jnp.einsum('ijd,de->ije', hidden_one, w_trunk_mid, preferred_element_type...  9.25 us
    ppermute x3, starting transfers between devices, ring_gather(): lax.ppermute(pieces[far - 1], axis, [(d, (d - 1) % ways) for d in range(w...  7.7 us
    pmax x1, blocking collectives, body(): row_peak = lax.pmax(jnp.max(scores, -1), 'col')  5.67 us
    dynamic_update_slice x6, other arithmetic, body(): lax.map(edge_block, (pair_embed.reshape(block_count, block_rows, key_coun...  5.22 us
    ppermute x3, waiting for transfers between devices, ring_gather(): lax.ppermute(pieces[far - 1], axis, [(d, (d - 1) % ways) for d in range(w...  4.99 us
  transfers between devices with their start and end apart: 4, of which 3 were waited for; matrix products, arithmetic and copies ran while one was open for 11% of the time, Pallas kernels for 0%

profile of v1, /device:TPU:0, one launch (start us, length us, event | category | flops | bytes accessed | tf_op | source)
XLA Modules:
  0.0 145.0 jit_solution(18346088553470720370)
XLA Ops:
  8.1 1.0 fusion.68
  9.9 5.0 %collective-permute-start = (bf16[48,256]{1,0:T(8,128)(2,1)S(1)}, bf16[48,256]{1,0:T(8,128)(2,1)S(1)}, u32[]{:S(2)}, u32[]{:S(2)}) collective-permute-start(bf16[48,256]{1,0:T(8,128)(2,1)S(1)} %add_convert_fusion), channel_id=1, source_target_pairs={{0,12},{4,0},{8,4},{12,8},{1,13},{5,1},{9,5},{13,9},{2,14},{6,2},{... | collective-permute-start | bytes 73736 | tf_op jit(solution)/shard_map/ppermute | solution.py:25
  17.5 1.0 fusion.69
  19.3 2.2 %convolution_convert_fusion.1 = bf16[48,2048]{1,0:T(8,128)(2,1)} fusion(bf16[48,256]{1,0:T(8,128)(2,1)S(1)} %add_convert_fusion, bf16[256,2048]{1,0:T(8,128)(2,1)} %param.32), kind=kOutput, calls=%fused_computation.30 | convolution fusion | flops 50429952 | bytes 1269760 | tf_op jit(solution)/shard_map/dot_general | solution.py:144
  24.0 3.4 %collective-permute-done.1 = bf16[48,256]{1,0:T(8,128)(2,1)S(1)} collective-permute-done((bf16[48,256]{1,0:T(8,128)(2,1)S(1)}, bf16[48,256]{1,0:T(8,128)(2,1)S(1)}, u32[]{:S(2)}, u32[]{:S(2)}) %collective-permute-start.1) | collective-permute-done | bytes 24608 | tf_op jit(solution)/shard_map/ppermute | solution.py:25
  27.4 2.2 %collective-permute-start.2 = (bf16[48,256]{1,0:T(8,128)(2,1)S(1)}, bf16[48,256]{1,0:T(8,128)(2,1)S(1)}, u32[]{:S(2)}, u32[]{:S(2)}) collective-permute-start(bf16[48,256]{1,0:T(8,128)(2,1)S(1)} %collective-permute-done.1), channel_id=1, source_target_pairs={{0,12},{4,0},{8,4},{12,8},{1,13},{5,1},{9,5},{13,9},{2,14},{6,2},{... | collective-permute-start | bytes 73736 | tf_op jit(solution)/shard_map/ppermute | solution.py:25
  29.6 1.6 %collective-permute-done.2 = bf16[48,256]{1,0:T(8,128)(2,1)S(1)} collective-permute-done((bf16[48,256]{1,0:T(8,128)(2,1)S(1)}, bf16[48,256]{1,0:T(8,128)(2,1)S(1)}, u32[]{:S(2)}, u32[]{:S(2)}) %collective-permute-start.2) | collective-permute-done | bytes 24608 | tf_op jit(solution)/shard_map/ppermute | solution.py:25
  31.9 1.1 fusion.50
  34.0 1.3 convolution_convert_fusion
  36.8 5.7 %pmax.7 = f32[8,48]{1,0:T(8,128)S(1)} all-reduce(f32[8,48]{1,0:T(8,128)S(1)} %get-tuple-element.115), channel_id=1, replica_groups=mesh['groups'=2,'row'=4,'col'=4] {'col'}, use_global_device_ids=true, to_apply=%region_1.2 | all-reduce | flops 384 | bytes 3072 | tf_op jit(solution)/shard_map/pmax | solution.py:183
  43.0 1.2 convolution_bitcast_fusion
  45.9 13.8 %all-reduce = (f32[48,8]{0,1:T(8,128)S(1)}, f32[48,3,8,12]{0,3,1,2:T(8,128)S(1)}) all-reduce(f32[48,8]{0,1:T(8,128)S(1)} %bitcast.172, f32[48,3,8,12]{0,3,1,2:T(8,128)S(1)} %convolution_bitcast_fusion.1), channel_id=1, replica_groups=mesh['groups'=2,'row'=4,'col'=4] {'col'}, use_global_device_ids=true, to_apply=%region_4.5 | all-reduce | flops 14208 | bytes 113664 | tf_op jit(solution)/shard_map/psum | solution.py:196
  60.4 1.8 %copy.97 = f32[48,3,8,12]{3,1,2,0:T(4,128)S(1)} copy(f32[48,3,8,12]{0,3,1,2:T(8,128)} %divide_subtract_fusion) | data formatting | bytes 110592 | tf_op jit(solution)/shard_map/sub | solution.py:75
  62.3 4.5 %multiply_reduce_fusion.1 = (f32[48,8,12]{2,1,0:T(8,128)}, bf16[48,3,8,12]{3,1,2,0:T(4,128)(2,1)}) fusion(f32[48,3,8,12]{3,1,2,0:T(4,128)S(1)} %copy.97, f32[3,3,48]{1,0,2:T(4,128)} %copy-done.5), kind=kOutput, calls=%fused_computation.51 | convolution fusion | flops 534528 | bytes 103104 | tf_op jit(solution)/shard_map/abi,iahv->ibhv/dot_general | solution.py:76
  67.1 1.1 copy.99
  68.3 1.5 %copy.98 = bf16[48,3,8,12]{0,3,2,1:T(8,128)(2,1)S(1)} copy(bf16[48,3,8,12]{3,1,2,0:T(4,128)(2,1)} %get-tuple-element.102) | data formatting | bytes 55296 | tf_op jit(solution)/shard_map/convert.5
  69.9 27.1 %all-reduce.4.cloned.1.call-done = (f32[48,2048]{1,0:T(8,128)}, f32[48,1024]{1,0:T(8,128)}) async-done(((f32[48,2048]{1,0:T(8,128)}, f32[48,1024]{1,0:T(8,128)}), (f32[48,2048]{1,0:T(8,128)}, f32[48,1024]{1,0:T(8,128)})) %all-reduce.4.cloned.1.call-update) | async-done | bytes 589840 | tf_op jit(solution)/shard_map/psum | solution.py:196
  97.1 1.0 fusion.29
  98.1 1.1 divide_convert_fusion
  99.3 2.0 %fusion.66 = (f32[48]{0:T(128)S(1)}, f32[48,256]{1,0:T(8,128)S(1)}) fusion(bf16[48,3456]{1,0:T(8,128)(2,1)S(1)} %concatenate.21, bf16[3456,256]{1,0:T(8,128)(2,1)} %param.39, bf16[48,256]{1,0:T(8,128)(2,1)S(1)} %add_convert_fusion), kind=kOutput, calls=%fused_computation.128 | convolution fusion | flops 84971472 | bytes 2175168 | tf_op jit(solution)/shard_map/dot_general | solution.py:88
  102.3 1.0 convolution_convert_fusion.2
  103.3 13.2 %all_gather.3 = bf16[192,128]{1,0:T(8,128)(2,1)S(1)} all-gather(bf16[48,128]{1,0:T(8,128)(2,1)S(1)} %convolution_convert_fusion.2), channel_id=1, replica_groups=mesh['groups'=2,'row'=4,'col'=4] {'row'}, dimensions={0}, use_global_device_ids=true | all-gather | bytes 61440 | tf_op jit(solution)/shard_map/all_gather | solution.py:211
  116.5 1.0 convolution_bitcast_fusion.3
  117.5 1.7 %fusion.44 = f32[48,384]{1,0:T(8,128)} fusion(bf16[48,128]{1,0:T(8,128)(2,1)S(1)} %get-tuple-element.215, bf16[384,384]{1,0:T(8,128)(2,1)} %param.43), kind=kOutput, calls=%fused_computation.74 | convolution fusion | flops 4718592 | bytes 184320 | tf_op jit(solution)/shard_map/dot_general | solution.py:215
  119.2 18.9 %while.10 = (s32[]{:T(128)}, bf16[6,8,48,128]{3,2,1,0:T(8,128)(2,1)}, bf16[6,8,48,128]{3,2,1,0:T(8,128)(2,1)S(1)}, bf16[384,384]{1,0:T(8,128)(2,1)}, f32[6,8,384...) while((s32[]{:T(128)}, ...), condition=%wide.region_15.16_spmd, body=%wide.region_12.15_spmd.sunk | while | flops 191054592 | bytes 2702265 | solution.py:246
  119.3 1.5 %fusion.111 = bf16[8,48,384]{2,1,0:T(8,128)(2,1)S(1)} fusion(bf16[8,48,128]{2,1,0:T(8,128)(2,1)S(1)} %dynamic-slice_bitcast_fusion.9, bf16[8,48,128]{2,1,0:T(8,128)(2,1)S(1)} %broadcast_in_dim.14, bf16[8,48,128]{2,1,0:T(8,128)(2,1)S(1)} %broadcast_in_dim.15, bf16[384,384]{1,0:T(8,128)(2,1)} %get-tuple-element.239, f32[48,384]{1,0:T(8,128)} %get-tuple-element.238, ...), kind=kOutput, calls=%fused_computation.6.clone.1 | convolution fusion | flops 152911872 | bytes 1167360 | tf_op jit(solution)/shard_map/while/body/eval_jaxpr/ijd,de->ije/dot_general | solution.py:231
  121.5 0.9 fusion.114
  122.5 1.5 %fusion.111 = bf16[8,48,384]{2,1,0:T(8,128)(2,1)S(1)} fusion(bf16[8,48,128]{2,1,0:T(8,128)(2,1)S(1)} %dynamic-slice_bitcast_fusion.9, bf16[8,48,128]{2,1,0:T(8,128)(2,1)S(1)} %broadcast_in_dim.14, bf16[8,48,128]{2,1,0:T(8,128)(2,1)S(1)} %broadcast_in_dim.15, bf16[384,384]{1,0:T(8,128)(2,1)} %get-tuple-element.239, f32[48,384]{1,0:T(8,128)} %get-tuple-element.238, ...), kind=kOutput, calls=%fused_computation.6.clone.1 | convolution fusion | flops 152911872 | bytes 1167360 | tf_op jit(solution)/shard_map/while/body/eval_jaxpr/ijd,de->ije/dot_general | solution.py:231
  125.6 1.5 %fusion.111 = bf16[8,48,384]{2,1,0:T(8,128)(2,1)S(1)} fusion(bf16[8,48,128]{2,1,0:T(8,128)(2,1)S(1)} %dynamic-slice_bitcast_fusion.9, bf16[8,48,128]{2,1,0:T(8,128)(2,1)S(1)} %broadcast_in_dim.14, bf16[8,48,128]{2,1,0:T(8,128)(2,1)S(1)} %broadcast_in_dim.15, bf16[384,384]{1,0:T(8,128)(2,1)} %get-tuple-element.239, f32[48,384]{1,0:T(8,128)} %get-tuple-element.238, ...), kind=kOutput, calls=%fused_computation.6.clone.1 | convolution fusion | flops 152911872 | bytes 1167360 | tf_op jit(solution)/shard_map/while/body/eval_jaxpr/ijd,de->ije/dot_general | solution.py:231
  128.8 1.5 %fusion.111 = bf16[8,48,384]{2,1,0:T(8,128)(2,1)S(1)} fusion(bf16[8,48,128]{2,1,0:T(8,128)(2,1)S(1)} %dynamic-slice_bitcast_fusion.9, bf16[8,48,128]{2,1,0:T(8,128)(2,1)S(1)} %broadcast_in_dim.14, bf16[8,48,128]{2,1,0:T(8,128)(2,1)S(1)} %broadcast_in_dim.15, bf16[384,384]{1,0:T(8,128)(2,1)} %get-tuple-element.239, f32[48,384]{1,0:T(8,128)} %get-tuple-element.238, ...), kind=kOutput, calls=%fused_computation.6.clone.1 | convolution fusion | flops 152911872 | bytes 1167360 | tf_op jit(solution)/shard_map/while/body/eval_jaxpr/ijd,de->ije/dot_general | solution.py:231
  131.9 1.5 %fusion.111 = bf16[8,48,384]{2,1,0:T(8,128)(2,1)S(1)} fusion(bf16[8,48,128]{2,1,0:T(8,128)(2,1)S(1)} %dynamic-slice_bitcast_fusion.9, bf16[8,48,128]{2,1,0:T(8,128)(2,1)S(1)} %broadcast_in_dim.14, bf16[8,48,128]{2,1,0:T(8,128)(2,1)S(1)} %broadcast_in_dim.15, bf16[384,384]{1,0:T(8,128)(2,1)} %get-tuple-element.239, f32[48,384]{1,0:T(8,128)} %get-tuple-element.238, ...), kind=kOutput, calls=%fused_computation.6.clone.1 | convolution fusion | flops 152911872 | bytes 1167360 | tf_op jit(solution)/shard_map/while/body/eval_jaxpr/ijd,de->ije/dot_general | solution.py:231
  135.1 1.5 %fusion.111 = bf16[8,48,384]{2,1,0:T(8,128)(2,1)S(1)} fusion(bf16[8,48,128]{2,1,0:T(8,128)(2,1)S(1)} %dynamic-slice_bitcast_fusion.9, bf16[8,48,128]{2,1,0:T(8,128)(2,1)S(1)} %broadcast_in_dim.14, bf16[8,48,128]{2,1,0:T(8,128)(2,1)S(1)} %broadcast_in_dim.15, bf16[384,384]{1,0:T(8,128)(2,1)} %get-tuple-element.239, f32[48,384]{1,0:T(8,128)} %get-tuple-element.238, ...), kind=kOutput, calls=%fused_computation.6.clone.1 | convolution fusion | flops 152911872 | bytes 1167360 | tf_op jit(solution)/shard_map/while/body/eval_jaxpr/ijd,de->ije/dot_general | solution.py:231
  (163 shorter events, 22.7 us)
Async XLA Ops:
  7.2 26.8 %copy-start = (bf16[256,4096]{1,0:T(8,128)(2,1)S(1)}, bf16[256,4096]{1,0:T(8,128)(2,1)}, u32[]{:S(2)}) copy-start(bf16[256,4096]{1,0:T(8,128)(2,1)} %param.34) | copy-start | bytes 6291460
  7.2 14.4 %copy-start.11 = (s32[192]{0:T(256)S(1)}, s32[192]{0:T(256)}, u32[]{:S(2)}) copy-start(s32[192]{0:T(256)} %param.29) | copy-start | bytes 2308
  7.2 14.4 %copy-start.12 = (s32[192]{0:T(256)S(1)}, s32[192]{0:T(256)}, u32[]{:S(2)}) copy-start(s32[192]{0:T(256)} %param.28) | copy-start | bytes 2308
  7.2 14.5 %copy-start.1 = (bf16[48,48,128]{2,1,0:T(8,128)(2,1)S(1)}, bf16[48,48,128]{2,1,0:T(8,128)(2,1)}, u32[]{:S(2)}) copy-start(bf16[48,48,128]{2,1,0:T(8,128)(2,1)} %param.27) | copy-start | bytes 1769476
  7.2 14.5 %copy-start.10 = (bf16[128,8]{0,1:T(8,128)(2,1)S(1)}, bf16[128,8]{0,1:T(8,128)(2,1)}, u32[]{:S(2)}) copy-start(bf16[128,8]{0,1:T(8,128)(2,1)} %param.36) | copy-start | bytes 6148
  7.2 89.8 %all-reduce.4.cloned.1.call-start = ((), (), s32[]{:S(2)}) async-start(), calls=%async_computation | async-start | bytes 1179648 | tf_op jit(solution)/shard_map/psum | solution.py:196
  9.9 13.6 %collective-permute-start = (bf16[48,256]{1,0:T(8,128)(2,1)S(1)}, bf16[48,256]{1,0:T(8,128)(2,1)S(1)}, u32[]{:S(2)}, u32[]{:S(2)}) collective-permute-start(bf16[48,256]{1,0:T(8,128)(2,1)S(1)} %add_convert_fusion), channel_id=1, source_target_pairs={{0,12},{4,0},{8,4},{12,8},{1,13},{5,1},{9,5},{13,9},{2,14},{6,2},{... | collective-permute-start | bytes 73736 | tf_op jit(solution)/shard_map/ppermute | solution.py:25
  18.7 2.9 %copy-start.5 = (f32[3,3,48]{1,0,2:T(4,128)}, f32[3,3,48]{1,0,2:T(4,128)S(1)}, u32[]{:S(2)}) copy-start(f32[3,3,48]{1,0,2:T(4,128)S(1)} %copy.125) | copy-start | bytes 5188
  23.6 3.8 %collective-permute-start.1 = (bf16[48,256]{1,0:T(8,128)(2,1)S(1)}, bf16[48,256]{1,0:T(8,128)(2,1)S(1)}, u32[]{:S(2)}, u32[]{:S(2)}) collective-permute-start(bf16[48,256]{1,0:T(8,128)(2,1)S(1)} %collective-permute-done), channel_id=1, source_target_pairs={{0,12},{4,0},{8,4},{12,8},{1,13},{5,1},{9,5},{13,9},{2,14},{6,2},{... | collective-permute-start | bytes 73736 | tf_op jit(solution)/shard_map/ppermute | solution.py:25
  27.4 3.8 %collective-permute-start.2 = (bf16[48,256]{1,0:T(8,128)(2,1)S(1)}, bf16[48,256]{1,0:T(8,128)(2,1)S(1)}, u32[]{:S(2)}, u32[]{:S(2)}) collective-permute-start(bf16[48,256]{1,0:T(8,128)(2,1)S(1)} %collective-permute-done.1), channel_id=1, source_target_pairs={{0,12},{4,0},{8,4},{12,8},{1,13},{5,1},{9,5},{13,9},{2,14},{6,2},{... | collective-permute-start | bytes 73736 | tf_op jit(solution)/shard_map/ppermute | solution.py:25
  31.3 0.7 copy-start.9
  33.9 2.7 %copy-start.13 = (f32[8]{0:T(128)S(1)}, f32[8]{0:T(128)}, u32[]{:S(2)}) copy-start(f32[8]{0:T(128)} %param.38) | copy-start | bytes 100
  33.9 2.6 %copy-start.3 = (bf16[48,2048]{1,0:T(8,128)(2,1)S(1)}, bf16[48,2048]{1,0:T(8,128)(2,1)}, u32[]{:S(2)}) copy-start(bf16[48,2048]{1,0:T(8,128)(2,1)} %convolution_convert_fusion.1) | copy-start | bytes 589828
  33.9 2.6 %copy-start.4 = (f32[8,48,48]{1,2,0:T(8,128)S(1)}, f32[8,48,48]{1,2,0:T(8,128)}, u32[]{:S(2)}) copy-start(f32[8,48,48]{1,2,0:T(8,128)} %copy.83) | copy-start | bytes 221188
  99.1 20.1 %copy-start.2 = (bf16[384,128]{1,0:T(8,128)(2,1)S(1)}, bf16[384,128]{1,0:T(8,128)(2,1)}, u32[]{:S(2)}) copy-start(bf16[384,128]{1,0:T(8,128)(2,1)} %param.45) | copy-start | bytes 294916
  99.3 2.4 %copy-start.6 = (bf16[256,256]{1,0:T(8,128)(2,1)S(1)}, bf16[256,256]{1,0:T(8,128)(2,1)}, u32[]{:S(2)}) copy-start(bf16[256,256]{1,0:T(8,128)(2,1)} %param.41) | copy-start | bytes 393220
  99.3 2.4 %copy-start.7 = (bf16[256,256]{1,0:T(8,128)(2,1)S(1)}, bf16[256,256]{1,0:T(8,128)(2,1)}, u32[]{:S(2)}) copy-start(bf16[256,256]{1,0:T(8,128)(2,1)} %param.40) | copy-start | bytes 393220
  102.3 16.9 %copy-start.8 = (bf16[48,256]{1,0:T(8,128)(2,1)}, bf16[48,256]{1,0:T(8,128)(2,1)S(1)}, u32[]{:S(2)}) copy-start(bf16[48,256]{1,0:T(8,128)(2,1)S(1)} %multiply_convert_fusion.1) | copy-start | bytes 73732
Sparse Core Ops, SparseCore 0:
  62.4 34.5 all-reduce.3
